TPU v7x, 32 devices: a whole 2x2x4 slice. The times are simulated.
32 devices in a mesh: dp: 16 (over z, x, core), mp: 2 (over y).
Axes of the slice: x: 2, y: 2, z: 4, core: 2. Of those that a mesh axis runs over, the one named last changes fastest.
Arguments:
- tokens: bfloat16 [2, 16, 448, 2048], P(None, 'dp'), may hold values from -6 to 6
- cotangent: bfloat16 [2, 16, 448, 2048], P(None, 'dp', None, 'mp'), may hold values from -6 to 6
- lengths: int32 [2, 16], P(None, 'dp'), may hold values from 1 to 448, as said below
- domains: int32 [2, 16, 1], P(None, 'dp'), may hold values from 0 to 7
- lower_bound: float32 [2048], replicated, may hold values from 0 to 1
- mixer_master: float32 [4, 2048, 2048], P(None, ('dp', 'mp')), may hold values from -0.125 to 0.125
- mixer_first: float32 [4, 2048, 2048], P(None, ('dp', 'mp'))
- mixer_second: float32 [4, 2048, 2048], P(None, ('dp', 'mp'))
- glu_in_master: float32 [2, 2048, 5632], P(None, 'dp', 'mp'), may hold values from -0.125 to 0.125
- glu_in_first: float32 [2, 2048, 5632], P(None, 'dp', 'mp')
- glu_in_second: float32 [2, 2048, 5632], P(None, 'dp', 'mp')
- glu_out_master: float32 [5632, 2048], P('mp', 'dp'), may hold values from -0.078125 to 0.078125
- glu_out_first: float32 [5632, 2048], P('mp', 'dp')
- glu_out_second: float32 [5632, 2048], P('mp', 'dp')
- gain_master: float32 [3, 2048], P(None, ('dp', 'mp')), may hold values from 0.5 to 1.5
- gain_first: float32 [3, 2048], P(None, ('dp', 'mp'))
- gain_second: float32 [3, 2048], P(None, ('dp', 'mp'))
Outputs:
- layer_out: bfloat16 [2, 16, 448, 2048], P(None, 'dp', None, 'mp')
- grad_tokens: bfloat16 [2, 16, 448, 2048], P(None, 'dp', None, 'mp')
- mixer_master_new: float32 [4, 2048, 2048], P(None, ('dp', 'mp'))
- mixer_first_new: float32 [4, 2048, 2048], P(None, ('dp', 'mp'))
- mixer_second_new: float32 [4, 2048, 2048], P(None, ('dp', 'mp'))
- glu_in_master_new: float32 [2, 2048, 5632], P(None, 'dp', 'mp')
- glu_in_first_new: float32 [2, 2048, 5632], P(None, 'dp', 'mp')
- glu_in_second_new: float32 [2, 2048, 5632], P(None, 'dp', 'mp')
- glu_out_master_new: float32 [5632, 2048], P('mp', 'dp')
- glu_out_first_new: float32 [5632, 2048], P('mp', 'dp')
- glu_out_second_new: float32 [5632, 2048], P('mp', 'dp')
- gain_master_new: float32 [3, 2048], P(None, ('dp', 'mp'))
- gain_first_new: float32 [3, 2048], P(None, ('dp', 'mp'))
- gain_second_new: float32 [3, 2048], P(None, ('dp', 'mp'))
Inputs may be any that keep to these rules, and one draw needn't show every extreme that they name: lengths rise from about a third of 448 at the first sequence index to 448 at the last; the last sequence of each micro-batch holds all 448 tokens.
All inputs are finite; a program needn't handle non-finite values.
Results may differ from a plain program's by a relative error of at most 0.023.
Values may be sent and summed in bfloat16 or wider, within the bound.
A program may use at most 296 MiB of HBM per device.

v0:
```python
import jax
import jax.numpy as jnp
from jax import lax
from jax.sharding import PartitionSpec as P

NDOM = 8
EPSILON = 1e-06
BETA_ONE = 0.9
BETA_TWO = 0.95
ADAM_EPSILON = 1e-08
DECAY_RATE = 0.1
MATRIX_RATE = 0.06
GAIN_RATE = 0.5
STEP_NUMBER = 3.0


def inverse_rms(values):
    return lax.rsqrt(jnp.mean(values * values, axis=-1, keepdims=True) + EPSILON)


def norm_back(grad_normed, unit_rows, inverse):
    return inverse * (
        grad_normed - unit_rows * jnp.mean(grad_normed * unit_rows, axis=-1, keepdims=True)
    )


def silu_slope(values):
    sigma = jax.nn.sigmoid(values)
    return sigma * (1.0 + values * (1.0 - sigma))


def linear_pair(earlier, later):
    return (earlier[0] * later[0], later[0] * earlier[1] + later[1])


def adamw_update(master, first, second, gradient, count, rate, decay):
    first_new = BETA_ONE * first + (1.0 - BETA_ONE) * gradient
    second_new = BETA_TWO * second + (1.0 - BETA_TWO) * gradient * gradient
    first_hat = first_new / (1.0 - BETA_ONE**count)
    second_hat = second_new / (1.0 - BETA_TWO**count)
    master_new = master - rate * (
        first_hat / (jnp.sqrt(second_hat) + ADAM_EPSILON) + decay * master
    )
    return (master_new, first_new, second_new)


def gather_weights(mixer_master, glu_in_master, glu_out_master, gain_master):
    mixer_full, gain_full = (
        lax.all_gather(mixer_master.astype(jnp.bfloat16), ("dp", "mp"), axis=1, tiled=True),
        lax.all_gather(gain_master.astype(jnp.bfloat16), ("dp", "mp"), axis=1, tiled=True),
    )
    glu_in_full, glu_out_full = (
        lax.all_gather(glu_in_master.astype(jnp.bfloat16), "dp", axis=1, tiled=True),
        lax.all_gather(glu_out_master.astype(jnp.bfloat16), "dp", axis=1, tiled=True),
    )
    return (mixer_full, gain_full.astype(jnp.float32), glu_in_full, glu_out_full)


def reduce_grads(mixer_grad, gain_grad, glu_in_grad, glu_out_grad):
    groups = lax.axis_size("dp")
    narrow = lax.axis_size("mp")
    mp_place = lax.axis_index("mp")
    full_width = mixer_grad.shape[2]
    row_count = full_width // (groups * narrow)
    mixer_pick = lax.dynamic_index_in_dim(
        mixer_grad.reshape(4, groups, narrow, row_count, full_width), mp_place, 2, keepdims=False
    )
    mixer_pick = mixer_pick.reshape(4, groups * row_count, full_width)
    gain_pick = lax.dynamic_index_in_dim(
        gain_grad.reshape(3, groups, narrow, row_count), mp_place, 2, keepdims=False
    )
    gain_pick = gain_pick.reshape(3, groups * row_count)
    mixer_own, gain_own = (
        lax.psum_scatter(
            mixer_pick.astype(jnp.bfloat16), "dp", scatter_dimension=1, tiled=True
        ).astype(jnp.float32),
        lax.psum_scatter(
            gain_pick.astype(jnp.bfloat16), "dp", scatter_dimension=1, tiled=True
        ).astype(jnp.float32),
    )
    glu_in_own, glu_out_own = (
        lax.psum_scatter(
            glu_in_grad.astype(jnp.bfloat16), "dp", scatter_dimension=1, tiled=True
        ).astype(jnp.float32),
        lax.psum_scatter(
            glu_out_grad.astype(jnp.bfloat16), "dp", scatter_dimension=1, tiled=True
        ).astype(jnp.float32),
    )
    return (mixer_own, gain_own, glu_in_own, glu_out_own)


def add_grads(first_set, second_set):
    return jax.tree.map(jnp.add, first_set, second_set)


def micro_batch(seq_in, cot_part, token_weight, lower_bound, weights_now):
    mixer_full, gain_full, glu_in_full, glu_out_full = weights_now
    mp_place = lax.axis_index("mp")
    part_width = cot_part.shape[1]
    inverse_in = inverse_rms(seq_in)
    unit_in = seq_in * inverse_in
    normed_in = (unit_in * gain_full[0]).astype(jnp.bfloat16)
    in_weights = mixer_full[:3]
    out_weight = mixer_full[3]
    state_gain = gain_full[1]
    pre_all = jnp.einsum("td,kde->kte", normed_in, in_weights, preferred_element_type=jnp.float32)
    pre_input = pre_all[0]
    pre_forget = pre_all[1]
    pre_gate = pre_all[2]
    forget_sig = jax.nn.sigmoid(pre_forget)
    forget = lower_bound + (1.0 - lower_bound) * forget_sig
    fresh_input = jax.nn.silu(pre_input)
    states = lax.associative_scan(linear_pair, (forget, (1.0 - forget) * fresh_input), axis=0)[1]
    inverse_state = inverse_rms(states)
    unit_state = states * inverse_state
    gate_act = jax.nn.silu(pre_gate)
    gated_out = (unit_state * state_gain * gate_act).astype(jnp.bfloat16)
    branch_mix = jnp.dot(gated_out, out_weight, preferred_element_type=jnp.float32)
    middle = seq_in + branch_mix
    inverse_mid = inverse_rms(middle)
    unit_mid = middle * inverse_mid
    normed_mid = (unit_mid * gain_full[2]).astype(jnp.bfloat16)
    pre_glu = jnp.einsum("td,kdf->ktf", normed_mid, glu_in_full, preferred_element_type=jnp.float32)
    act_part = jax.nn.silu(pre_glu[0])
    hidden = (act_part * pre_glu[1]).astype(jnp.bfloat16)
    partial_out = jnp.dot(hidden, glu_out_full, preferred_element_type=jnp.float32)
    branch = lax.psum_scatter(
        partial_out.astype(jnp.bfloat16), "mp", scatter_dimension=1, tiled=True
    ).astype(jnp.float32)
    output = (
        lax.dynamic_slice_in_dim(middle, mp_place * part_width, part_width, 1) + branch
    ).astype(jnp.bfloat16)
    cot_full = lax.all_gather(cot_part, "mp", axis=1, tiled=True)
    back = cot_full.astype(jnp.float32) * token_weight[:, None]
    back_low = back.astype(jnp.bfloat16)
    grad_glu_out = jnp.einsum("tf,td->fd", hidden, back_low, preferred_element_type=jnp.float32)
    grad_hidden = jnp.einsum(
        "td,fd->tf", back_low, glu_out_full, preferred_element_type=jnp.float32
    )
    grad_pre_glu = jnp.stack(
        [grad_hidden * pre_glu[1] * silu_slope(pre_glu[0]), grad_hidden * act_part]
    ).astype(jnp.bfloat16)
    grad_glu_in = jnp.einsum(
        "td,ktf->kdf", normed_mid, grad_pre_glu, preferred_element_type=jnp.float32
    )
    grad_normed_part = jnp.einsum(
        "ktf,kdf->td", grad_pre_glu, glu_in_full, preferred_element_type=jnp.float32
    )
    grad_normed_mid = lax.psum(grad_normed_part, "mp")
    gain_mid = jnp.sum(grad_normed_mid * unit_mid, axis=0)
    grad_middle = back + norm_back(grad_normed_mid * gain_full[2], unit_mid, inverse_mid)
    middle_low = grad_middle.astype(jnp.bfloat16)
    grad_mix_out = jnp.einsum(
        "td,te->de", gated_out, middle_low, preferred_element_type=jnp.float32
    )
    grad_gated = jnp.einsum("te,de->td", middle_low, out_weight, preferred_element_type=jnp.float32)
    gain_state = jnp.sum(grad_gated * unit_state * gate_act, axis=0)
    grad_pre_gate = grad_gated * unit_state * state_gain * silu_slope(pre_gate)
    scaled_grad = grad_gated * state_gain * gate_act
    grad_states = norm_back(scaled_grad, unit_state, inverse_state)
    next_forget = jnp.concatenate([forget[1:], jnp.zeros_like(forget[:1])], axis=0)
    carried = lax.associative_scan(linear_pair, (next_forget, grad_states), reverse=True, axis=0)[1]
    earlier_states = jnp.concatenate([jnp.zeros_like(states[:1]), states[:-1]], axis=0)
    grad_forget = carried * (earlier_states - fresh_input)
    grad_fresh = carried * (1.0 - forget)
    grad_pre = jnp.stack(
        [
            grad_fresh * silu_slope(pre_input),
            grad_forget * (1.0 - lower_bound) * forget_sig * (1.0 - forget_sig),
            grad_pre_gate,
        ]
    ).astype(jnp.bfloat16)
    grad_mix_in = jnp.einsum("td,kte->kde", normed_in, grad_pre, preferred_element_type=jnp.float32)
    grad_normed_in = jnp.einsum(
        "kte,kde->td", grad_pre, in_weights, preferred_element_type=jnp.float32
    )
    gain_in = jnp.sum(grad_normed_in * unit_in, axis=0)
    grad_seq = grad_middle + norm_back(grad_normed_in * gain_full[0], unit_in, inverse_in)
    grad_slice = lax.dynamic_slice_in_dim(grad_seq, mp_place * part_width, part_width, 1).astype(
        jnp.bfloat16
    )
    mixer_grad = jnp.concatenate([grad_mix_in, grad_mix_out[None]], axis=0)
    gain_grad = jnp.stack([gain_in, gain_state, gain_mid])
    return (output, grad_slice, (mixer_grad, gain_grad, grad_glu_in, grad_glu_out))


def shards(
    tokens,
    cotangent,
    lengths,
    domains,
    lower_bound,
    mixer_master,
    mixer_first,
    mixer_second,
    glu_in_master,
    glu_in_first,
    glu_in_second,
    glu_out_master,
    glu_out_first,
    glu_out_second,
    gain_master,
    gain_first,
    gain_second,
):
    batches = tokens.shape[0]
    seq_len = tokens.shape[2]
    groups = lax.axis_size("dp")
    domain_ids = jnp.arange(NDOM, dtype=jnp.int32)
    member = (domains[..., 0][..., None] == domain_ids).astype(jnp.float32)
    live_counts = lengths.astype(jnp.float32)
    counts, token_total = lax.psum(
        (jnp.sum(member * live_counts[..., None], axis=(0, 1)), jnp.sum(live_counts)), "dp"
    )
    seq_weight = token_total / (NDOM * jnp.sum(member * counts, axis=-1))
    positions = jnp.arange(seq_len, dtype=jnp.int32)
    outputs = []
    grad_rows = []
    totals = None
    for batch_index in range(batches):
        weights_now = gather_weights(mixer_master, glu_in_master, glu_out_master, gain_master)
        token_weight = seq_weight[batch_index, 0] * (positions < lengths[batch_index, 0]).astype(
            jnp.float32
        )
        output, grad_slice, local_grads = micro_batch(
            tokens[batch_index, 0].astype(jnp.float32),
            cotangent[batch_index, 0],
            token_weight,
            lower_bound,
            weights_now,
        )
        outputs.append(output)
        grad_rows.append(grad_slice)
        totals = local_grads if totals is None else add_grads(totals, local_grads)
    totals = reduce_grads(totals[0], totals[1], totals[2], totals[3])
    scale_factor = 1.0 / (batches * groups * tokens.shape[1])
    count = STEP_NUMBER
    mixer_new = adamw_update(
        mixer_master,
        mixer_first,
        mixer_second,
        totals[0] * scale_factor,
        count,
        MATRIX_RATE,
        DECAY_RATE,
    )
    gain_new = adamw_update(
        gain_master, gain_first, gain_second, totals[1] * scale_factor, count, GAIN_RATE, 0.0
    )
    glu_in_new = adamw_update(
        glu_in_master,
        glu_in_first,
        glu_in_second,
        totals[2] * scale_factor,
        count,
        MATRIX_RATE,
        DECAY_RATE,
    )
    glu_out_new = adamw_update(
        glu_out_master,
        glu_out_first,
        glu_out_second,
        totals[3] * scale_factor,
        count,
        MATRIX_RATE,
        DECAY_RATE,
    )
    layer_out = jnp.stack(outputs)[:, None]
    grad_tokens = jnp.stack(grad_rows)[:, None]
    return (
        layer_out,
        grad_tokens,
        mixer_new[0],
        mixer_new[1],
        mixer_new[2],
        glu_in_new[0],
        glu_in_new[1],
        glu_in_new[2],
        glu_out_new[0],
        glu_out_new[1],
        glu_out_new[2],
        gain_new[0],
        gain_new[1],
        gain_new[2],
    )


def solution(mesh):
    in_specs = (
        P(None, "dp", None, None),
        P(None, "dp", None, "mp"),
        P(None, "dp"),
        P(None, "dp", None),
        P(),
        P(None, ("dp", "mp"), None),
        P(None, ("dp", "mp"), None),
        P(None, ("dp", "mp"), None),
        P(None, "dp", "mp"),
        P(None, "dp", "mp"),
        P(None, "dp", "mp"),
        P("mp", "dp"),
        P("mp", "dp"),
        P("mp", "dp"),
        P(None, ("dp", "mp")),
        P(None, ("dp", "mp")),
        P(None, ("dp", "mp")),
    )
    out_specs = (
        P(None, "dp", None, "mp"),
        P(None, "dp", None, "mp"),
        P(None, ("dp", "mp"), None),
        P(None, ("dp", "mp"), None),
        P(None, ("dp", "mp"), None),
        P(None, "dp", "mp"),
        P(None, "dp", "mp"),
        P(None, "dp", "mp"),
        P("mp", "dp"),
        P("mp", "dp"),
        P("mp", "dp"),
        P(None, ("dp", "mp")),
        P(None, ("dp", "mp")),
        P(None, ("dp", "mp")),
    )
    return jax.shard_map(shards, mesh=mesh, in_specs=in_specs, out_specs=out_specs, check_vma=False)
```

profile of v0, /device:TPU:0, one launch (start us, length us, event | category | flops | bytes accessed | tf_op | source)
XLA Modules:
  0.0 1983.9 jit_solution(1037557350118298409)
XLA Ops:
  17.5 36.6 %all-reduce.68 = (f32[8]{0:T(128)S(1)}, f32[]{:T(128)}) all-reduce(f32[8]{0:T(128)S(1)} %select_reduce_fusion.1, f32[]{:T(128)} %convert_reduce_fusion), channel_id=1, replica_groups=mesh['dp'=16,'mp'=2] {'dp'}, use_global_device_ids=true, to_apply=%region_11.12 | all-reduce | flops 9 | bytes 72 | tf_op jit(solution)/shard_map/psum | solution.py:212
  58.6 66.2 %all-gather.2 = bf16[32,64,3]{1,2,0:T(4,128)(2,1)S(1)} all-gather(bf16[1,64,3]{1,2,0:T(4,128)(2,1)S(1)} %convert_bitcast_fusion), channel_id=1, replica_groups=mesh['dp'=16,'mp'=2] {'dp','mp'}, dimensions={0}, use_global_device_ids=true | all-gather | bytes 12672 | tf_op jit(solution)/shard_map/all_gather | solution.py:50
  129.3 80.2 %all-gather.9.cloned.1.call-done = bf16[4,2048,2048]{2,1,0:T(8,128)(2,1)} async-done(((bf16[4,64,2048]{2,1,0:T(8,128)(2,1)}), bf16[4,2048,2048]{2,1,0:T(8,128)(2,1)}) %all-gather.9.cloned.1.call-update) | async-done | bytes 33554448 | tf_op jit(solution)/shard_map/all_gather | solution.py:49
  209.5 19.6 fusion.22
  229.1 19.6 fusion.19
  248.7 10.2 subtract_multiply_fusion.3
  521.0 10.3 pad.231
  553.9 10.5 multiply_reduce_fusion.12
  573.9 18.9 convolution_bitcast_fusion
  592.8 14.9 fusion.56
  607.7 17.8 fusion.49
  625.4 19.0 convolution_bitcast_fusion.1
  644.5 14.9 fusion.55
  659.4 17.8 fusion.48
  747.8 16.4 slice.1030
  764.1 16.8 slice.1021
  780.9 10.6 slice.1023
  791.5 16.5 slice.1101
  808.0 16.7 slice.1092
  824.7 10.6 slice.1094
  843.9 11.0 convolution_convert_fusion.1
  855.0 12.9 fusion.97
  880.9 10.7 fusion.13
  891.7 16.1 multiply_reduce_fusion.3
  907.7 11.1 subtract_multiply_fusion.1
  945.0 16.4 slice.1025
  961.3 10.7 slice.1027
  1046.4 16.4 slice.1096
  1062.8 10.6 slice.1098
  1130.1 10.8 slice.1084
  1184.3 32.1 %rev.4 = f32[448,2048]{1,0:T(8,128)} reverse(f32[448,2048]{1,0:T(8,128)} %add.764), dimensions={0} | reverse | bytes 7340032 | tf_op jit(solution)/shard_map/rev | solution.py:162
  1216.6 10.8 slice.1155
  1248.5 10.2 pad.263
  1264.6 32.2 %rev.5 = f32[448,2048]{1,0:T(8,128)} reverse(f32[448,2048]{1,0:T(8,128)} %add.793), dimensions={0} | reverse | bytes 7340032 | tf_op jit(solution)/shard_map/rev | solution.py:162
  1305.9 18.9 fusion.7
  1329.9 22.6 %fusion.39 = (f32[2048]{0:T(1024)S(1)}, f32[448]{0:T(512)}, f32[448]{0:T(512)}, f32[2048]{0:T(1024)S(1)}, f32[448,2048]{1,0:T(8,128)}, /*index=5*/f32[448,2048]{1,0:T(8,128)}, f32[448,2048]{1,0:T(8,128)}, f32[448,2048]{1,0:T(8,128)}) fusion(f32[448]{0:T(512)S(1)} %copy-done.132, bf16[2,1,448,2048]{3,2,1,0:T(8,128)(2,1)} %param.17, f32[448]{0:T(512)S(1)} %copy-done.129, ...), kind=kOutput, calls=%fused_computation.81 | convolution fusion | flops 11292635136 | bytes 52722688 | tf_op jit(solution)/shard_map/kte,kde->td/dot_general | solution.py:174
  1353.8 14.6 add_convert_fusion.1
  1368.4 15.5 copy.92
  1384.0 13.1 fusion.94
  1405.6 25.0 %fusion.58 = f32[3,2048,2048]{1,2,0:T(8,128)} fusion(bf16[1,448,2048]{2,1,0:T(8,128)(2,1)S(1)} %copy-done.53, bf16[1,448,2048]{2,1,0:T(8,128)(2,1)S(1)} %copy-done.39, bf16[1,448,2048]{2,1,0:T(8,128)(2,1)S(1)} %copy-done.38, f32[2048]{0:T(1024)S(1)} %bitcast.323, f32[448]{0:T(512)S(1)} %copy-done.129, bf16[2,1,448,2048]{3,2,1,0:T(8,128)(2,1)S(1)} %copy-done.31), kind=kOutput, calls=%fused_computation.148 | convolution fusion | flops 11283464192 | bytes 57681920 | tf_op jit(solution)/shard_map/td,kte->kde/dot_general | solution.py:173
  1430.6 21.7 %fusion.57 = f32[3,2048,2048]{1,2,0:T(8,128)} fusion(bf16[1,448,2048]{2,1,0:T(8,128)(2,1)S(1)} %copy-done.52, bf16[1,448,2048]{2,1,0:T(8,128)(2,1)S(1)} %copy-done.41, bf16[1,448,2048]{2,1,0:T(8,128)(2,1)S(1)} %copy-done.40, f32[448]{0:T(512)S(1)} %copy-done.132, f32[2048]{0:T(1024)S(1)} %bitcast.324, bf16[2,1,448,2048]{3,2,1,0:T(8,128)(2,1)S(1)} %copy-done.31), kind=kOutput, calls=%fused_computation.147 | convolution fusion | flops 11283464192 | bytes 57681920 | tf_op jit(solution)/shard_map/td,kte->kde/dot_general | solution.py:173
  1452.3 28.1 %fusion.2 = bf16[4,16,1,64,2048]{4,3,2,1,0:T(8,128)(2,1)} fusion(s32[]{:T(128)S(6)} %select_n.13, f32[3,16,2,64,2048]{4,3,2,1,0:T(8,128)} %bitcast.297, f32[1,16,2,64,2048]{4,3,2,1,0:T(8,128)} %bitcast.304, f32[3,16,2,64,2048]{4,3,2,1,0:T(8,128)} %bitcast.296, f32[1,16,2,64,2048]{4,3,2,1,0:T(8,128)} %bitcast.303), kind=kLoop, calls=%fused_computation.7 | loop fusion | flops 33554432 | bytes 150994944 | tf_op jit(solution)/shard_map/convert_element_type | solution.py:75
  1481.0 24.5 %fusion.46 = f32[2,2816,2048]{2,1,0:T(8,128)} fusion(bf16[1,448,2816]{2,1,0:T(8,128)(2,1)} %get-tuple-element.161, bf16[1,448,2816]{2,1,0:T(8,128)(2,1)} %get-tuple-element.160, f32[448,2048]{1,0:T(8,128)} %get-tuple-element.253, f32[2048]{0:T(1024)S(1)} %bitcast.313, f32[448]{0:T(512)S(1)} %copy-done.119), kind=kOutput, calls=%fused_computation.128 | convolution fusion | flops 10340040704 | bytes 54863616 | tf_op jit(solution)/shard_map/td,ktf->kdf/dot_general | solution.py:143
  1505.6 27.1 %fusion.4 = bf16[2,2048,2816]{1,2,0:T(8,128)(2,1)} fusion(f32[2,2816,2048]{2,1,0:T(8,128)} %fusion.46, bf16[1,448,2816]{2,1,0:T(8,128)(2,1)} %get-tuple-element.163, bf16[1,448,2816]{2,1,0:T(8,128)(2,1)S(1)} %copy-done.149, f32[448,2048]{1,0:T(8,128)} %get-tuple-element.251, f32[448]{0:T(512)S(1)} %copy-done.126, f32[2048]{0:T(1024)S(1)} %bitcast.314), kind=kOutput, calls=%fused_computation.9 | convolution fusion | flops 10363109376 | bytes 77932288 | tf_op jit(solution)/shard_map/td,ktf->kdf/dot_general | solution.py:143
  1532.6 57.8 %copy.90 = bf16[2,2048,2816]{2,0,1:T(2,128)(2,1)} copy(bf16[2,2048,2816]{1,2,0:T(8,128)(2,1)} %fusion.4) | data formatting | bytes 46137344
  1590.4 24.4 %copy.97 = bf16[256,8,2,2816]{3,1,2,0:T(8,128)(2,1)} copy(bf16[256,8,2,2816]{3,2,1,0:T(2,128)(2,1)} %bitcast.294) | data formatting | bytes 46137344
  1647.8 72.6 %reduce-scatter.17.cloned.1.call-done = bf16[4,64,2048]{2,1,0:T(8,128)(2,1)} async-done(((bf16[4,1024,2048]{2,1,0:T(8,128)(2,1)}), bf16[4,64,2048]{2,1,0:T(8,128)(2,1)}) %reduce-scatter.17.cloned.1.call-update) | async-done | bytes 1048592 | tf_op jit(solution)/shard_map/reduce_scatter | solution.py:74
  1727.5 222.8 %reduce-scatter.19.cloned.1.call-done = bf16[128,5632]{1,0:T(8,128)(2,1)} async-done(((bf16[2048,5632]{1,0:T(8,128)(2,1)}), bf16[128,5632]{1,0:T(8,128)(2,1)}) %reduce-scatter.19.cloned.1.call-update) | async-done | bytes 1441808
  (794 shorter events, 721.9 us)
Async XLA Ops:
  7.2 202.3 %all-gather.9.cloned.1.call-start = ((), (), s32[]{:S(2)}) async-start(), calls=%async_computation.6 | async-start | bytes 34603008 | tf_op jit(solution)/shard_map/all_gather | solution.py:49
  10.1 563.7 %all-gather.11.cloned.1.call-start = ((), (), s32[]{:S(2)}) async-start(), calls=%async_computation.7 | async-start | bytes 24510464 | tf_op jit(solution)/shard_map/all_gather | solution.py:53
  11.5 44.0 %copy-start.135 = (f32[3,64]{1,0:T(4,128)S(1)}, f32[3,64]{1,0:T(4,128)}, u32[]{:S(2)}) copy-start(f32[3,64]{1,0:T(4,128)} %param.31) | copy-start | bytes 2308
  11.5 581.2 %all-gather.17.cloned.1.call-start = ((), (), s32[]{:S(2)}) async-start(), calls=%async_computation.13 | async-start | bytes 2752512 | tf_op jit(solution)/shard_map/all_gather | solution.py:133
  14.5 44.0 %copy-start.97 = (f32[2048]{0:T(1024)S(1)}, f32[2048]{0:T(1024)}, u32[]{:S(2)}) copy-start(f32[2048]{0:T(1024)} %param.21) | copy-start | bytes 24580
  14.5 578.2 %all-gather.13.cloned.1.call-start = ((), (), s32[]{:S(2)}) async-start(), calls=%async_computation.8 | async-start | bytes 12255232 | tf_op jit(solution)/shard_map/all_gather | solution.py:54
  15.6 628.9 %all-gather.15.cloned.1.call-start = ((), (), s32[]{:S(2)}) async-start(), calls=%async_computation.12 | async-start | bytes 2752512 | tf_op jit(solution)/shard_map/all_gather | solution.py:133
  16.2 851.8 %all-reduce.72.cloned.1.call-start = ((), (), s32[]{:S(2)}) async-start(), calls=%async_computation.17 | async-start | bytes 14680064 | tf_op jit(solution)/shard_map/psum | solution.py:149
  58.6 190.2 %copy-start.71 = (f32[2048]{0:T(1024)}, f32[2048]{0:T(1024)S(1)}, u32[]{:S(2)}) copy-start(f32[2048]{0:T(1024)S(1)} %broadcast_subtract_fusion) | copy-start | bytes 24580
  125.5 103.6 %copy-start.137 = (f32[1,2048]{1,0:T(1,128)}, f32[1,2048]{1,0:T(1,128)S(1)}, u32[]{:S(2)}) copy-start(f32[1,2048]{1,0:T(1,128)S(1)} %get-tuple-element.233) | copy-start | bytes 24580
  125.5 422.4 %copy-start.93 = (f32[1,2048]{1,0:T(1,128)}, f32[1,2048]{1,0:T(1,128)S(1)}, u32[]{:S(2)}) copy-start(f32[1,2048]{1,0:T(1,128)S(1)} %get-tuple-element.232) | copy-start | bytes 24580
  129.3 99.8 %copy-start.131 = (f32[448]{0:T(512)}, f32[448]{0:T(512)S(1)}, u32[]{:S(2)}) copy-start(f32[448]{0:T(512)S(1)} %get-tuple-element.255) | copy-start | bytes 5380
  129.3 99.8 %copy-start.128 = (f32[448]{0:T(512)}, f32[448]{0:T(512)S(1)}, u32[]{:S(2)}) copy-start(f32[448]{0:T(512)S(1)} %get-tuple-element.256) | copy-start | bytes 5380
  449.6 17.0 copy-start.87
  449.6 17.0 copy-start.88
  449.6 17.0 copy-start.89
  449.6 17.0 copy-start.90
  450.4 16.4 copy-start.77
  450.4 16.4 copy-start.78
  564.4 308.5 %copy-start.118 = (f32[448]{0:T(512)}, f32[448]{0:T(512)S(1)}, u32[]{:S(2)}) copy-start(f32[448]{0:T(512)S(1)} %add_rsqrt_fusion.3) | copy-start | bytes 5380
  573.8 18.9 copy-start.124
  573.9 18.9 copy-start.139
  625.4 19.0 copy-start.127
  677.2 946.9 %reduce-scatter.15.cloned.1.call-start = ((), (), s32[]{:S(2)}) async-start(), calls=%async_computation.10 | async-start | bytes 2752512 | tf_op jit(solution)/shard_map/reduce_scatter | solution.py:127
  687.2 940.0 %reduce-scatter.13.cloned.1.call-start = ((), (), s32[]{:S(2)}) async-start(), calls=%async_computation.9 | async-start | bytes 2752512 | tf_op jit(solution)/shard_map/reduce_scatter | solution.py:127
  791.5 33.3 %copy-start.24 = (f32[224,2048]{1,0:T(8,128)S(1)}, f32[224,2048]{1,0:T(8,128)}, u32[]{:S(2)}) copy-start(f32[224,2048]{1,0:T(8,128)} %slice.1093) | copy-start | bytes 5505028
  855.0 783.9 %reduce-scatter.23.cloned.1.call-start = ((), (), s32[]{:S(2)}) async-start(), calls=%async_computation.16 | async-start | bytes 278528
  1130.1 17.6 copy-start.55
  1130.1 17.6 copy-start.57
  1184.3 32.1 %copy-start.22 = (f32[223,2048]{1,0:T(8,128)S(1)}, f32[223,2048]{1,0:T(8,128)}, u32[]{:S(2)}) copy-start(f32[223,2048]{1,0:T(8,128)} %slice.1154) | copy-start | bytes 5480452
  1264.6 32.3 %copy-start.72 = (f32[2048]{0:T(1024)S(1)}, f32[2048]{0:T(1024)}, u32[]{:S(2)}) copy-start(f32[2048]{0:T(1024)} %copy-done.71) | copy-start | bytes 24580
  1296.8 28.0 %slice-start.3 = ((s8[11010048]{0:T(1024)(128)(4,1)}), s8[4194304]{0:T(1024)(128)(4,1)S(1)}, s32[]{:S(2)}) async-start(s8[11010048]{0:T(1024)(128)(4,1)} %bitcast.301), calls=%async_computation.21 | async-start | bytes 8388608
  1305.9 18.9 copy-start.37
  1305.9 18.9 copy-start
  1305.9 18.9 slice-start.4
  1305.9 18.9 slice-start.5
  1305.9 18.9 copy-start.13
  1305.9 18.9 copy-start.14
  1329.9 23.9 %copy-start.50 = (bf16[1,1,448,2048]{3,2,1,0:T(8,128)(2,1)S(1)}, bf16[1,1,448,2048]{3,2,1,0:T(8,128)(2,1)}, u32[]{:S(2)}) copy-start(bf16[1,1,448,2048]{3,2,1,0:T(8,128)(2,1)} %all-gather.17.cloned.1.call-done) | copy-start | bytes 5505028
  1329.9 23.9 %copy-start.141 = (f32[448]{0:T(512)S(1)}, f32[448]{0:T(512)}, u32[]{:S(2)}) copy-start(f32[448]{0:T(512)} %fusion.132) | copy-start | bytes 5380
  1353.7 286.6 %reduce-scatter.21.cloned.1.call-start = ((), (), s32[]{:S(2)}) async-start(), calls=%async_computation.15 | async-start | bytes 12255232
  1383.9 336.5 %reduce-scatter.17.cloned.1.call-start = ((), (), s32[]{:S(2)}) async-start(), calls=%async_computation.11 | async-start | bytes 17825792 | tf_op jit(solution)/shard_map/reduce_scatter | solution.py:74
  1405.6 25.0 %copy-start.40 = (bf16[1,448,2048]{2,1,0:T(8,128)(2,1)S(1)}, bf16[1,448,2048]{2,1,0:T(8,128)(2,1)}, u32[]{:S(2)}) copy-start(bf16[1,448,2048]{2,1,0:T(8,128)(2,1)} %get-tuple-element.166) | copy-start | bytes 5505028
  1405.6 25.0 %copy-start.41 = (bf16[1,448,2048]{2,1,0:T(8,128)(2,1)S(1)}, bf16[1,448,2048]{2,1,0:T(8,128)(2,1)}, u32[]{:S(2)}) copy-start(bf16[1,448,2048]{2,1,0:T(8,128)(2,1)} %get-tuple-element.167) | copy-start | bytes 5505028
  1405.6 25.0 %copy-start.52 = (bf16[1,448,2048]{2,1,0:T(8,128)(2,1)S(1)}, bf16[1,448,2048]{2,1,0:T(8,128)(2,1)}, u32[]{:S(2)}) copy-start(bf16[1,448,2048]{2,1,0:T(8,128)(2,1)} %get-tuple-element.239) | copy-start | bytes 5505028
  1480.3 25.2 %copy-start.126 = (f32[448]{0:T(512)S(1)}, f32[448]{0:T(512)}, u32[]{:S(2)}) copy-start(f32[448]{0:T(512)} %copy-done.124) | copy-start | bytes 5380
  1480.4 25.2 %copy-start.149 = (bf16[1,448,2816]{2,1,0:T(8,128)(2,1)S(1)}, bf16[1,448,2816]{2,1,0:T(8,128)(2,1)}, u32[]{:S(2)}) copy-start(bf16[1,448,2816]{2,1,0:T(8,128)(2,1)} %get-tuple-element.162) | copy-start | bytes 7569412
  1480.4 469.9 %reduce-scatter.19.cloned.1.call-start = ((), (), s32[]{:S(2)}) async-start(), calls=%async_computation.14 | async-start | bytes 24510464
  (120 other events, 786.7 us)
Sparse Core Ops, SparseCore 0:
  11.7 197.7 all-gather.8
  211.6 116.8 all-gather.10
  330.1 30.1 all-gather.16
  362.3 97.3 all-gather.12
  461.1 28.3 all-gather.14
  677.3 174.8 all-reduce.71
  855.1 28.9 reduce-scatter.14
  886.9 28.9 reduce-scatter.12
  1353.8 54.1 reduce-scatter.22
  1412.6 125.2 reduce-scatter.20
  1542.0 178.3 reduce-scatter.16
  1724.4 225.8 reduce-scatter.18
where the time goes:
time: 2010 us; the launch traced here: 1980 us
  local copies, waits for them, and re-layouts  851 us (42%)
  matrix products  399 us (20%)
  waiting for transfers between devices  376 us (19%)
  other arithmetic  236 us (12%)
  blocking collectives  103 us (5%)
    slice x110, local copies, waits for them, and re-layouts, micro_batch(): lax.associative_scan(linear_pair, (next_forget, grad_states), reverse=Tru...  349 us
    unnamed x15, waiting for transfers between devices  223 us
    slice x98, local copies, waits for them, and re-layouts, micro_batch(): lax.associative_scan(linear_pair, (forget, (1.0 - forget) * fresh_input),...  188 us
    unnamed x326, local copies, waits for them, and re-layouts  140 us
    all_gather x1, waiting for transfers between devices, gather_weights(): lax.all_gather(mixer_master.astype(jnp.bfloat16), ('dp', 'mp'), axis=1, t...  80.2 us
    reduce_scatter x1, waiting for transfers between devices, reduce_grads(): lax.psum_scatter(mixer_pick.astype(jnp.bfloat16), 'dp', scatter_dimension...  72.6 us
    all_gather x1, blocking collectives, gather_weights(): lax.all_gather(gain_master.astype(jnp.bfloat16), ('dp', 'mp'), axis=1, ti...  66.2 us
    rev x2, local copies, waits for them, and re-layouts, micro_batch(): lax.associative_scan(linear_pair, (next_forget, grad_states), reverse=Tru...  64.4 us
  transfers between devices with their start and end apart: 12, of which 3 were waited for; matrix products, arithmetic and copies ran while one was open for 71% of the time, Pallas kernels for 0%

commit v1 on v0

--- a/solution.py
+++ b/solution.py
@@ -14,6 +14,28 @@
 STEP_NUMBER = 3.0
 
 
+def in_order(tiles, dim):
+    tiles = jnp.moveaxis(tiles, 0, dim)
+    lengths = tiles.shape
+    return tiles.reshape(*lengths[:dim], lengths[dim] * lengths[dim + 1], *lengths[dim + 2 :])
+
+
+def collected_by_bits(array, axis):
+    size = lax.axis_size(axis)
+    blocks = array[None]
+    for level in range(size.bit_length() - 1):
+        apart = 1 << level
+        theirs = lax.ppermute(blocks, axis, [(i, i ^ apart) for i in range(size)])
+        both = jnp.stack([blocks, theirs])
+        upper = lax.axis_index(axis) >> level & 1
+        blocks = jnp.where(upper == 0, both, both[::-1]).reshape(-1, *array.shape)
+    return blocks
+
+
+def gather_by_bits(x, axis, dim):
+    return in_order(collected_by_bits(x, axis), dim)
+
+
 def inverse_rms(values):
     return lax.rsqrt(jnp.mean(values * values, axis=-1, keepdims=True) + EPSILON)
 
@@ -46,7 +68,7 @@
 
 def gather_weights(mixer_master, glu_in_master, glu_out_master, gain_master):
     mixer_full, gain_full = (
-        lax.all_gather(mixer_master.astype(jnp.bfloat16), ("dp", "mp"), axis=1, tiled=True),
+        gather_by_bits(mixer_master.astype(jnp.bfloat16), ("dp", "mp"), 1),
         lax.all_gather(gain_master.astype(jnp.bfloat16), ("dp", "mp"), axis=1, tiled=True),
     )
     glu_in_full, glu_out_full = (

time: 2010 us -> 3210 us (1.60)
  blocking collectives: 103 us -> 798 us
  waiting for transfers between devices: 376 us -> 735 us
  other arithmetic: 236 us -> 345 us
  local copies, waits for them, and re-layouts: 851 us -> 887 us
    psum x1, blocking collectives: 36.6 us -> 729 us  [shards(): lax.psum((jnp.sum(member * live_counts[..., None], axis=(0, 1)), jnp.sum(...]
    ppermute x0 -> x5, waiting for transfers between devices: none -> 445 us  [collected_by_bits(): theirs = lax.ppermute(blocks, axis, [(i, i ^ apart) for i in range(size)])]
    all_gather x1 -> x0, waiting for transfers between devices: 80.2 us -> none  [gather_weights(): lax.all_gather(mixer_master.astype(jnp.bfloat16), ('dp', 'mp'), axis=1, t...]
    select_n x0 -> x4, other arithmetic: none -> 58.2 us  [collected_by_bits(): blocks = jnp.where(upper == 0, both, both[::-1]).reshape(-1, *array.shape)]
    another operation x0 -> x7, other arithmetic: none -> 44.1 us  [collected_by_bits(): both = jnp.stack([blocks, theirs])]
    unnamed x326 -> x324, local copies, waits for them, and re-layouts: 140 us -> 142 us
    unnamed x15 -> x14, waiting for transfers between devices: 223 us -> 223 us
  transfers between devices with their start and end apart: 12 -> 16, of which waited for: 3 -> 6; matrix products, arithmetic and copies ran while one was open for 71% -> 49% of each run, Pallas kernels for 0% -> 0%
where the time goes in v1:
time: 3210 us; the launch traced here: 3180 us
  local copies, waits for them, and re-layouts  887 us (28%)
  blocking collectives  798 us (25%)
  waiting for transfers between devices  735 us (23%)
  matrix products  388 us (12%)
  other arithmetic  345 us (11%)
    psum x1, blocking collectives, shards(): lax.psum((jnp.sum(member * live_counts[..., None], axis=(0, 1)), jnp.sum(...  729 us
    ppermute x5, waiting for transfers between devices, collected_by_bits(): theirs = lax.ppermute(blocks, axis, [(i, i ^ apart) for i in range(size)])  445 us
    slice x110, local copies, waits for them, and re-layouts, micro_batch(): lax.associative_scan(linear_pair, (next_forget, grad_states), reverse=Tru...  349 us
    unnamed x14, waiting for transfers between devices  223 us
    slice x98, local copies, waits for them, and re-layouts, micro_batch(): lax.associative_scan(linear_pair, (forget, (1.0 - forget) * fresh_input),...  187 us
    unnamed x324, local copies, waits for them, and re-layouts  142 us
    all_gather x1, blocking collectives, gather_weights(): lax.all_gather(gain_master.astype(jnp.bfloat16), ('dp', 'mp'), axis=1, ti...  69 us
    reduce_scatter x1, waiting for transfers between devices, reduce_grads(): lax.psum_scatter(mixer_pick.astype(jnp.bfloat16), 'dp', scatter_dimension...  66.7 us
  transfers between devices with their start and end apart: 16, of which 6 were waited for; matrix products, arithmetic and copies ran while one was open for 49% of the time, Pallas kernels for 0%

profile of v1, /device:TPU:0, one launch (start us, length us, event | category | flops | bytes accessed | tf_op | source)
XLA Modules:
  0.0 3177.4 jit_solution(12895554561586082294)
XLA Ops:
  14.7 23.4 collective-permute-done
  51.8 168.2 %collective-permute-done.2 = bf16[4,4,64,2048]{3,2,1,0:T(8,128)(2,1)} collective-permute-done((bf16[4,4,64,2048]{3,2,1,0:T(8,128)(2,1)}, bf16[4,4,64,2048]{3,2,1,0:T(8,128)(2,1)}, u32[]{:S(2)}, u32[]{:S(2)}) %collective-permute-start.2) | collective-permute-done | bytes 4194336 | tf_op jit(solution)/shard_map/ppermute | solution.py:28
  227.5 14.6 reverse_select_fusion.2
  245.1 249.1 %collective-permute-done.3 = bf16[8,4,64,2048]{3,2,1,0:T(8,128)(2,1)} collective-permute-done((bf16[8,4,64,2048]{3,2,1,0:T(8,128)(2,1)}, bf16[8,4,64,2048]{3,2,1,0:T(8,128)(2,1)}, u32[]{:S(2)}, u32[]{:S(2)}) %collective-permute-start.3) | collective-permute-done | bytes 8388640 | tf_op jit(solution)/shard_map/ppermute | solution.py:28
  519.2 728.6 %all-reduce.68 = (f32[8]{0:T(128)S(1)}, f32[]{:T(128)}) all-reduce(f32[8]{0:T(128)S(1)} %select_reduce_fusion.1, f32[]{:T(128)} %convert_reduce_fusion), channel_id=1, replica_groups=mesh['dp'=16,'mp'=2] {'dp'}, use_global_device_ids=true, to_apply=%region_11.12 | all-reduce | flops 9 | bytes 72 | tf_op jit(solution)/shard_map/psum | solution.py:234
  1247.9 69.0 %all-gather.2 = bf16[32,64,3]{1,2,0:T(4,128)(2,1)S(1)} all-gather(bf16[1,64,3]{1,2,0:T(4,128)(2,1)S(1)} %convert_bitcast_fusion.4), channel_id=1, replica_groups=mesh['dp'=16,'mp'=2] {'dp','mp'}, dimensions={0}, use_global_device_ids=true | all-gather | bytes 12672 | tf_op jit(solution)/shard_map/all_gather | solution.py:72
  1326.2 23.1 pad_maximum_fusion
  1349.4 33.0 %reverse_select_fusion = bf16[2,16,4,64,2048]{4,3,1,0,2:T(8,128)(2,1)} fusion(bf16[2,16,4,64,2048]{4,3,1,0,2:T(8,128)(2,1)} %pad_maximum_fusion, pred[]{:T(512)S(6)} %eq.47), kind=kLoop, calls=%fused_computation.4 | loop fusion | flops 16777216 | bytes 67108864 | tf_op jit(solution)/shard_map/jit(_where)/select_n | solution.py:31
  1390.6 21.4 slice.1163
  1412.0 19.0 convolution_bitcast_fusion.3
  1431.0 15.6 convolution_bitcast_fusion.2
  1446.6 11.7 subtract_multiply_fusion.3
  1765.4 18.8 convolution_bitcast_fusion
  1784.2 15.2 fusion.48
  1799.4 17.8 fusion.41
  1817.2 19.0 convolution_bitcast_fusion.1
  1836.3 15.0 fusion.47
  1851.3 17.8 fusion.40
  1869.1 11.1 convolution_convert_fusion
  1940.9 16.3 slice.1035
  1957.2 16.9 slice.1026
  1984.7 16.5 slice.1106
  2001.2 16.7 slice.1097
  2017.9 10.7 slice.1099
  2037.3 11.0 convolution_convert_fusion.1
  2048.5 12.9 fusion.109
  2084.3 15.7 multiply_reduce_fusion.3
  2099.9 11.1 subtract_multiply_fusion.1
  2137.3 16.3 slice.1030
  2238.6 16.3 slice.1101
  2322.3 10.8 slice.1089
  2376.8 32.1 %rev.35 = f32[448,2048]{1,0:T(8,128)} reverse(f32[448,2048]{1,0:T(8,128)} %add.777), dimensions={0} | reverse | bytes 7340032 | tf_op jit(solution)/shard_map/rev | solution.py:184
  2409.1 10.8 slice.1160
  2456.8 32.2 %rev.36 = f32[448,2048]{1,0:T(8,128)} reverse(f32[448,2048]{1,0:T(8,128)} %add.806), dimensions={0} | reverse | bytes 7340032 | tf_op jit(solution)/shard_map/rev | solution.py:184
  2498.3 19.8 fusion.52
  2526.6 22.6 fusion.31
  2550.5 14.7 add_convert_fusion.1
  2565.2 15.7 copy.104
  2581.0 13.1 fusion.105
  2602.6 26.8 fusion.51
  2629.4 22.2 fusion.49
  2651.6 28.0 fusion.2
  2680.3 24.8 fusion.38
  2705.1 27.1 fusion.4
  2732.2 57.6 %copy.102 = bf16[2,2048,2816]{2,0,1:T(2,128)(2,1)} copy(bf16[2,2048,2816]{1,2,0:T(8,128)(2,1)} %fusion.4) | data formatting | bytes 46137344
  2789.9 24.4 copy.109
  2847.4 66.7 %reduce-scatter.17.cloned.1.call-done = bf16[4,64,2048]{2,1,0:T(8,128)(2,1)} async-done(((bf16[4,1024,2048]{2,1,0:T(8,128)(2,1)}), bf16[4,64,2048]{2,1,0:T(8,128)(2,1)}) %reduce-scatter.17.cloned.1.call-update) | async-done | bytes 1048592 | tf_op jit(solution)/shard_map/reduce_scatter | solution.py:96
  2921.1 223.0 %reduce-scatter.19.cloned.1.call-done = bf16[128,5632]{1,0:T(8,128)(2,1)} async-done(((bf16[2048,5632]{1,0:T(8,128)(2,1)}), bf16[128,5632]{1,0:T(8,128)(2,1)}) %reduce-scatter.19.cloned.1.call-update) | async-done | bytes 1441808
  (813 shorter events, 835.8 us)
Async XLA Ops:
  7.2 1758.2 %all-gather.8.cloned.1.call-start = ((), (), s32[]{:S(2)}) async-start(), calls=%async_computation.6 | async-start | bytes 24510464 | tf_op jit(solution)/shard_map/all_gather | solution.py:75
  10.5 1773.8 %all-gather.14.cloned.1.call-start = ((), (), s32[]{:S(2)}) async-start(), calls=%async_computation.12 | async-start | bytes 2752512 | tf_op jit(solution)/shard_map/all_gather | solution.py:155
  11.8 26.3 collective-permute-start
  40.3 4.5 collective-permute-start.1
  50.0 169.9 %collective-permute-start.2 = (bf16[4,4,64,2048]{3,2,1,0:T(8,128)(2,1)}, bf16[4,4,64,2048]{3,2,1,0:T(8,128)(2,1)}, u32[]{:S(2)}, u32[]{:S(2)}) collective-permute-start(bf16[4,4,64,2048]{3,2,1,0:T(8,128)(2,1)} %bitcast.8), channel_id=1, source_target_pairs={{0,4},{1,5},{2,6},{3,7},{4,0},{5,1},{6,2},{7,3},{8,12},{9,13},{10,... | collective-permute-start | bytes 12582920 | tf_op jit(solution)/shard_map/ppermute | solution.py:28
  242.1 252.1 %collective-permute-start.3 = (bf16[8,4,64,2048]{3,2,1,0:T(8,128)(2,1)}, bf16[8,4,64,2048]{3,2,1,0:T(8,128)(2,1)}, u32[]{:S(2)}, u32[]{:S(2)}) collective-permute-start(bf16[8,4,64,2048]{3,2,1,0:T(8,128)(2,1)} %bitcast.345), channel_id=1, source_target_pairs={{0,8},{1,9},{2,10},{3,11},{4,12},{5,13},{6,14},{7,15},{8,0},{9,1},... | collective-permute-start | bytes 25165832 | tf_op jit(solution)/shard_map/ppermute | solution.py:28
  243.5 1540.7 %all-gather.10.cloned.1.call-start = ((), (), s32[]{:S(2)}) async-start(), calls=%async_computation.7 | async-start | bytes 12255232 | tf_op jit(solution)/shard_map/all_gather | solution.py:76
  245.1 1591.2 %all-gather.12.cloned.1.call-start = ((), (), s32[]{:S(2)}) async-start(), calls=%async_computation.11 | async-start | bytes 2752512 | tf_op jit(solution)/shard_map/all_gather | solution.py:155
  509.7 738.2 %copy-start.133 = (f32[3,64]{1,0:T(4,128)S(1)}, f32[3,64]{1,0:T(4,128)}, u32[]{:S(2)}) copy-start(f32[3,64]{1,0:T(4,128)} %param.31) | copy-start | bytes 2308
  516.4 809.2 %copy-start.96 = (f32[2048]{0:T(1024)S(1)}, f32[2048]{0:T(1024)}, u32[]{:S(2)}) copy-start(f32[2048]{0:T(1024)} %param.21) | copy-start | bytes 24580
  516.4 809.8 %collective-permute-start.4 = (bf16[16,4,64,2048]{3,2,0,1:T(8,128)(2,1)}, bf16[16,4,64,2048]{3,2,0,1:T(8,128)(2,1)}, u32[]{:S(2)}, u32[]{:S(2)}) collective-permute-start(bf16[16,4,64,2048]{3,2,0,1:T(8,128)(2,1)} %bitcast.14), channel_id=1, source_target_pairs={{0,16},{1,17},{2,18},{3,19},{4,20},{5,21},{6,22},{7,23},{8,24},{9,... | collective-permute-start | bytes 50331656 | tf_op jit(solution)/shard_map/ppermute | solution.py:28
  519.2 1542.2 %all-reduce.72.cloned.1.call-start = ((), (), s32[]{:S(2)}) async-start(), calls=%async_computation.16 | async-start | bytes 14680064 | tf_op jit(solution)/shard_map/psum | solution.py:171
  1325.5 86.5 %copy-start.126 = (f32[448]{0:T(512)}, f32[448]{0:T(512)S(1)}, u32[]{:S(2)}) copy-start(f32[448]{0:T(512)S(1)} %get-tuple-element.260) | copy-start | bytes 5380
  1325.5 105.4 %copy-start.129 = (f32[448]{0:T(512)}, f32[448]{0:T(512)S(1)}, u32[]{:S(2)}) copy-start(f32[448]{0:T(512)S(1)} %get-tuple-element.259) | copy-start | bytes 5380
  1325.6 121.1 %copy-start.70 = (f32[2048]{0:T(1024)}, f32[2048]{0:T(1024)S(1)}, u32[]{:S(2)}) copy-start(f32[2048]{0:T(1024)S(1)} %broadcast_subtract_fusion) | copy-start | bytes 24580
  1326.2 104.8 %copy-start.135 = (f32[1,2048]{1,0:T(1,128)}, f32[1,2048]{1,0:T(1,128)S(1)}, u32[]{:S(2)}) copy-start(f32[1,2048]{1,0:T(1,128)S(1)} %get-tuple-element.237) | copy-start | bytes 24580
  1390.6 21.4 copy-start.28
  1647.8 17.0 copy-start.86
  1647.8 17.0 copy-start.87
  1647.8 17.0 copy-start.88
  1759.3 307.0 %copy-start.116 = (f32[448]{0:T(512)}, f32[448]{0:T(512)S(1)}, u32[]{:S(2)}) copy-start(f32[448]{0:T(512)S(1)} %add_rsqrt_fusion.3) | copy-start | bytes 5380
  1765.4 18.8 copy-start.122
  1765.4 18.8 copy-start.137
  1817.2 19.0 copy-start.125
  1869.1 954.6 %reduce-scatter.15.cloned.1.call-start = ((), (), s32[]{:S(2)}) async-start(), calls=%async_computation.9 | async-start | bytes 2752512 | tf_op jit(solution)/shard_map/reduce_scatter | solution.py:149
  1880.3 946.5 %reduce-scatter.13.cloned.1.call-start = ((), (), s32[]{:S(2)}) async-start(), calls=%async_computation.8 | async-start | bytes 2752512 | tf_op jit(solution)/shard_map/reduce_scatter | solution.py:149
  1984.7 33.2 %copy-start.22 = (f32[224,2048]{1,0:T(8,128)S(1)}, f32[224,2048]{1,0:T(8,128)}, u32[]{:S(2)}) copy-start(f32[224,2048]{1,0:T(8,128)} %slice.1098) | copy-start | bytes 5505028
  2048.4 790.1 %reduce-scatter.23.cloned.1.call-start = ((), (), s32[]{:S(2)}) async-start(), calls=%async_computation.15 | async-start | bytes 278528
  2048.4 17.9 copy-start.123
  2322.3 17.6 copy-start.54
  2322.3 17.6 copy-start.56
  2376.8 32.2 %copy-start.20 = (f32[223,2048]{1,0:T(8,128)S(1)}, f32[223,2048]{1,0:T(8,128)}, u32[]{:S(2)}) copy-start(f32[223,2048]{1,0:T(8,128)} %slice.1159) | copy-start | bytes 5480452
  2376.8 43.0 %copy-start.78 = (f32[3,2048]{1,0:T(4,128)S(1)}, f32[3,2048]{1,0:T(4,128)}, u32[]{:S(2)}) copy-start(f32[3,2048]{1,0:T(4,128)} %slice.1142) | copy-start | bytes 73732
  2376.8 43.0 %copy-start.79 = (f32[3,2048]{1,0:T(4,128)S(1)}, f32[3,2048]{1,0:T(4,128)}, u32[]{:S(2)}) copy-start(f32[3,2048]{1,0:T(4,128)} %slice.1138) | copy-start | bytes 73732
  2376.8 43.0 %copy-start.80 = (f32[3,2048]{1,0:T(4,128)S(1)}, f32[3,2048]{1,0:T(4,128)}, u32[]{:S(2)}) copy-start(f32[3,2048]{1,0:T(4,128)} %slice.1140) | copy-start | bytes 73732
  2376.8 43.0 %copy-start.81 = (f32[3,2048]{1,0:T(4,128)S(1)}, f32[3,2048]{1,0:T(4,128)}, u32[]{:S(2)}) copy-start(f32[3,2048]{1,0:T(4,128)} %slice.1139) | copy-start | bytes 73732
  2456.8 32.2 %copy-start.71 = (f32[2048]{0:T(1024)S(1)}, f32[2048]{0:T(1024)}, u32[]{:S(2)}) copy-start(f32[2048]{0:T(1024)} %copy-done.70) | copy-start | bytes 24580
  2498.3 19.8 copy-start
  2526.6 23.9 copy-start.49
  2526.6 23.9 copy-start.139
  2550.4 289.5 %reduce-scatter.21.cloned.1.call-start = ((), (), s32[]{:S(2)}) async-start(), calls=%async_computation.14 | async-start | bytes 12255232
  2580.9 333.1 %reduce-scatter.17.cloned.1.call-start = ((), (), s32[]{:S(2)}) async-start(), calls=%async_computation.10 | async-start | bytes 17825792 | tf_op jit(solution)/shard_map/reduce_scatter | solution.py:96
  2602.6 26.8 copy-start.38
  2602.6 26.8 copy-start.39
  2602.6 26.8 copy-start.51
  2679.6 25.5 copy-start.124
  2679.6 25.5 copy-start.147
  2679.6 464.5 %reduce-scatter.19.cloned.1.call-start = ((), (), s32[]{:S(2)}) async-start(), calls=%async_computation.13 | async-start | bytes 24510464
  (123 other events, 847.1 us)
Sparse Core Ops, SparseCore 0:
  10.6 198.0 all-gather.7
  243.7 30.7 all-gather.13
  276.6 156.0 all-gather.9
  519.3 28.6 all-gather.11
  1869.2 172.0 all-reduce.71
  2044.1 28.9 reduce-scatter.14
  2075.9 28.9 reduce-scatter.12
  2550.5 51.1 reduce-scatter.22
  2606.4 125.2 reduce-scatter.20
  2735.6 178.4 reduce-scatter.16
  2918.2 225.8 reduce-scatter.18
